TPU v7x, 32 devices: a whole 2x2x4 slice. The times are simulated.
32 devices in a mesh: groups: 2 (over x), ctx: 16 (over z, y, core).
Axes of the slice: x: 2, y: 2, z: 4, core: 2. Of those that a mesh axis runs over, the one named last changes fastest.
Arguments:
- q_span: bfloat16 [2048, 8192], P(('groups', 'ctx')), parts along dimension 0, may hold values from -200 to 200
- k_span: bfloat16 [2048, 1024], P(('groups', 'ctx')), parts along dimension 0, may hold values from -30 to 30
- v_span: bfloat16 [2048, 1024], P(('groups', 'ctx')), parts along dimension 0, may hold values from -6 to 6
- k_prefix: bfloat16 [1024, 1024], P(('groups', 'ctx')), parts along dimension 0, may hold values from -30 to 30
- v_prefix: bfloat16 [1024, 1024], P(('groups', 'ctx')), parts along dimension 0, may hold values from -6 to 6
- start_offset: int32 [2], P('groups'), parts along dimension 0, may hold values from 0 to 511
- prefix_len: int32 [2], P('groups'), parts along dimension 0, may hold values from 1 to 512
- block_order: int32 [64], P('groups'), parts along dimension 0, may hold values from 0 to 31, each once
Outputs:
- attended: bfloat16 [2048, 8192], P(('groups', 'ctx')), parts along dimension 0
There are 2 independent parts, one for each index of `groups`. A program takes and returns all parts, laid end to end along the dimension named above; each array names one. Nothing has to cross between parts.
All inputs are finite; a program needn't handle non-finite values.
Results may differ from a plain program's by a relative error of at most 0.006.
Values may be sent and summed in bfloat16 or wider, within the bound.
A program may use at most 128 MiB of HBM per device.

v0:
```python
import math

import jax
import jax.numpy as jnp
from jax import lax
from jax.sharding import PartitionSpec as P

HD = 128


NEG_FILL = -1e30


def local(q_span, k_span, v_span, k_prefix, v_prefix, start_offset, prefix_len, block_order):
    local_rows = q_span.shape[0]
    block_rows = local_rows // 2
    kv_heads = k_span.shape[1] // HD
    q_heads = q_span.shape[1] // HD
    table_len = block_order.shape[0]
    offset_value = start_offset[0]
    prefix_valid = prefix_len[0]
    scaling = 1.0 / math.sqrt(HD)
    members = lax.axis_size("ctx")
    heads_here = q_heads // members
    spread = members // kv_heads

    def widen(source):
        length = source.shape[0]
        grown = jnp.broadcast_to(
            source.reshape(length, kv_heads, 1, HD), (length, kv_heads, spread, HD)
        )
        return grown.reshape(length, members, HD)

    q_send = q_span.reshape(local_rows, members, heads_here * HD)
    q_whole, kc_whole, vc_whole, kp_whole, vp_whole = (
        lax.all_to_all(q_send, "ctx", split_axis=1, concat_axis=0, tiled=True),
        lax.all_to_all(widen(k_span), "ctx", split_axis=1, concat_axis=0, tiled=True),
        lax.all_to_all(widen(v_span), "ctx", split_axis=1, concat_axis=0, tiled=True),
        lax.all_to_all(widen(k_prefix), "ctx", split_axis=1, concat_axis=0, tiled=True),
        lax.all_to_all(widen(v_prefix), "ctx", split_axis=1, concat_axis=0, tiled=True),
    )
    whole_rows = q_whole.shape[0]
    prefix_whole = kp_whole.shape[0]
    key_stack = jnp.concatenate([kp_whole, kc_whole], 0).reshape(prefix_whole + whole_rows, HD)
    value_stack = jnp.concatenate([vp_whole, vc_whole], 0).reshape(prefix_whole + whole_rows, HD)
    row_index = jnp.arange(whole_rows, dtype=jnp.int32)
    which_block = row_index // block_rows
    matches = which_block[:, None] == jnp.arange(table_len, dtype=jnp.int32)[None, :]
    placed = jnp.sum(jnp.where(matches, block_order[None, :], 0), axis=1)
    all_pos = placed * block_rows + row_index % block_rows
    prefix_open = jnp.arange(prefix_whole, dtype=jnp.int32) < prefix_valid
    block_size = math.gcd(whole_rows, 512)
    block_count = whole_rows // block_size

    def head_block(packed):
        query_rows, query_place = packed
        scores = (
            jnp.einsum("qhd,kd->hqk", query_rows, key_stack, preferred_element_type=jnp.float32)
            * scaling
        )
        causal = (all_pos[None, :] <= query_place[:, None]) & (all_pos[None, :] >= offset_value)
        visible = jnp.concatenate(
            [jnp.broadcast_to(prefix_open[None, :], (block_size, prefix_whole)), causal], 1
        )
        scores = jnp.where(visible[None], scores, NEG_FILL)
        largest = jnp.max(scores, axis=-1, keepdims=True)
        weights = jnp.where(visible[None], jnp.exp(scores - largest), 0.0)
        denominator = jnp.sum(weights, axis=-1)
        summed = jnp.einsum(
            "hqk,kd->qhd",
            weights.astype(jnp.bfloat16),
            value_stack,
            preferred_element_type=jnp.float32,
        )
        result = summed / denominator.T[..., None]
        return result.reshape(block_size, heads_here * HD).astype(jnp.bfloat16)

    outputs = lax.map(
        head_block,
        (
            q_whole.reshape(block_count, block_size, heads_here, HD),
            all_pos.reshape(block_count, block_size),
        ),
    )
    outputs = outputs.reshape(whole_rows, 1, heads_here * HD)
    returned = lax.all_to_all(outputs, "ctx", split_axis=0, concat_axis=1, tiled=True)
    return returned.reshape(local_rows, q_heads * HD)


def solution(mesh):
    placed = (
        P(("groups", "ctx"), None),
        P(("groups", "ctx"), None),
        P(("groups", "ctx"), None),
        P(("groups", "ctx"), None),
        P(("groups", "ctx"), None),
        P("groups"),
        P("groups"),
        P("groups"),
    )
    return jax.shard_map(
        local, mesh=mesh, in_specs=placed, out_specs=P(("groups", "ctx"), None), check_vma=False
    )
```

profile of v0, /device:TPU:0, one launch (start us, length us, event | category | flops | bytes accessed | tf_op | source)
XLA Modules:
  0.0 155.1 jit_solution(3690061197051776769)
XLA Ops:
  0.0 0.0 copy-start
  0.0 0.0 copy-start.1
  0.0 0.9 copy_bitcast_fusion.10
  0.9 0.7 broadcast_in_dim.89
  1.6 7.4 %all-to-all-start.3 = ((bf16[32,16,128]{2,0,1:T(8,128)(2,1)}), bf16[32,16,128]{2,0,1:T(8,128)(2,1)S(1)}, u32[]{:S(2)}, u32[]{:S(2)}) async-start(bf16[32,16,128]{2,0,1:T(8,128)(2,1)} %bitcast.12), calls=%async_computation.3 | async-start | bytes 262144 | tf_op jit(solution)/shard_map/all_to_all | solution.py:40
  9.0 0.9 copy_bitcast_fusion.11
  9.8 7.1 %all-to-all-done.3 = bf16[32,16,128]{2,0,1:T(8,128)(2,1)S(1)} async-done(((bf16[32,16,128]{2,0,1:T(8,128)(2,1)}), bf16[32,16,128]{2,0,1:T(8,128)(2,1)S(1)}, u32[]{:S(2)}, u32[]{:S(2)}) %all-to-all-start.3) | async-done | bytes 131104 | tf_op jit(solution)/shard_map/all_to_all | solution.py:40
  16.9 0.7 broadcast_in_dim.85
  17.6 3.5 %all-to-all-start.1 = ((bf16[32,16,128]{2,0,1:T(8,128)(2,1)}), bf16[32,16,128]{2,0,1:T(8,128)(2,1)S(1)}, u32[]{:S(2)}, u32[]{:S(2)}) async-start(bf16[32,16,128]{2,0,1:T(8,128)(2,1)} %bitcast.3), calls=%async_computation.1 | async-start | bytes 262144 | tf_op jit(solution)/shard_map/all_to_all | solution.py:39
  21.1 0.0 copy-done
  21.1 7.9 %all-to-all-done.1 = bf16[32,16,128]{2,0,1:T(8,128)(2,1)S(1)} async-done(((bf16[32,16,128]{2,0,1:T(8,128)(2,1)}), bf16[32,16,128]{2,0,1:T(8,128)(2,1)S(1)}, u32[]{:S(2)}, u32[]{:S(2)}) %all-to-all-start.1) | async-done | bytes 131104 | tf_op jit(solution)/shard_map/all_to_all | solution.py:39
  29.0 0.8 broadcast_in_dim.91
  29.7 3.5 %all-to-all-start.4 = ((bf16[64,16,128]{2,0,1:T(8,128)(2,1)}), bf16[64,16,128]{2,0,1:T(8,128)(2,1)S(1)}, u32[]{:S(2)}, u32[]{:S(2)}) async-start(bf16[64,16,128]{2,0,1:T(8,128)(2,1)} %bitcast.16), calls=%async_computation.4 | async-start | bytes 524288 | tf_op jit(solution)/shard_map/all_to_all | solution.py:38
  33.3 0.9 copy_bitcast_fusion.9
  34.2 9.1 %all-to-all-done.4 = bf16[64,16,128]{2,0,1:T(8,128)(2,1)S(1)} async-done(((bf16[64,16,128]{2,0,1:T(8,128)(2,1)}), bf16[64,16,128]{2,0,1:T(8,128)(2,1)S(1)}, u32[]{:S(2)}, u32[]{:S(2)}) %all-to-all-start.4) | async-done | bytes 262176 | tf_op jit(solution)/shard_map/all_to_all | solution.py:38
  43.3 0.7 broadcast_in_dim.87
  44.0 3.5 %all-to-all-start.2 = ((bf16[64,16,128]{2,0,1:T(8,128)(2,1)}), bf16[64,16,128]{2,0,1:T(8,128)(2,1)S(1)}, u32[]{:S(2)}, u32[]{:S(2)}) async-start(bf16[64,16,128]{2,0,1:T(8,128)(2,1)} %bitcast.7), calls=%async_computation.2 | async-start | bytes 524288 | tf_op jit(solution)/shard_map/all_to_all | solution.py:37
  47.6 2.3 %copy.77 = bf16[8,16,8,512]{3,2,0,1:T(8,128)(2,1)} copy(bf16[8,16,8,512]{3,2,1,0:T(8,128)(2,1)} %bitcast.144) | data formatting | bytes 2097152 | tf_op jit(solution)/shard_map/reshape | solution.py:34
  49.9 7.7 %all-to-all-done.2 = bf16[64,16,128]{2,0,1:T(8,128)(2,1)S(1)} async-done(((bf16[64,16,128]{2,0,1:T(8,128)(2,1)}), bf16[64,16,128]{2,0,1:T(8,128)(2,1)S(1)}, u32[]{:S(2)}, u32[]{:S(2)}) %all-to-all-start.2) | async-done | bytes 262176 | tf_op jit(solution)/shard_map/all_to_all | solution.py:37
  57.6 3.7 %all-to-all-start = ((bf16[64,16,512]{2,0,1:T(8,128)(2,1)}), bf16[64,16,512]{2,0,1:T(8,128)(2,1)S(1)}, u32[]{:S(2)}, u32[]{:S(2)}) async-start(bf16[64,16,512]{2,0,1:T(8,128)(2,1)} %bitcast.119), calls=%async_computation | async-start | bytes 2097152 | tf_op jit(solution)/shard_map/all_to_all | solution.py:36
  61.3 0.0 copy-done.1
  61.3 0.1 select_reduce_fusion
  61.4 0.9 copy.46
  62.4 0.8 maximum_bitcast_fusion
  63.2 21.0 %all-to-all-done = bf16[64,16,512]{2,0,1:T(8,128)(2,1)S(1)} async-done(((bf16[64,16,512]{2,0,1:T(8,128)(2,1)}), bf16[64,16,512]{2,0,1:T(8,128)(2,1)S(1)}, u32[]{:S(2)}, u32[]{:S(2)}) %all-to-all-start) | async-done | bytes 1048608 | tf_op jit(solution)/shard_map/all_to_all | solution.py:36
  84.1 0.3 reshape.83
  84.4 34.0 %while.11 = (s32[]{:T(128)}, bf16[2,512,512]{2,1,0:T(8,128)(2,1)S(1)}, s32[1024]{0:T(1024)S(1)}, s32[2,512]{1,0:T(2,128)S(1)}, s32[]{:T(128)}, /*index=5*/bf16[2...) while((s32[]{:T(128)}, ...), condition=%wide.region_4.5_spmd.clone, body=%wide.region_1.4_spmd.clone.sunk | while | flops 1631849472 | bytes 20222080 | solution.py:78
  84.4 0.7 broadcast_compare_fusion.2
  85.1 0.4 compare_and_fusion.2
  85.5 0.7 iota_compare_fusion.3
  86.2 0.3 pad_add_fusion.2
  86.5 0.2 constant_dynamic-slice_fusion.5
  86.7 9.5 %fusion.60 = (f32[4,512]{1,0:T(4,128)S(1)}, bf16[4,512,1536]{2,1,0:T(8,128)(2,1)}) fusion(pred[512,1536]{1,0:T(8,128)(4,1)S(1)} %pad_add_fusion.2, bf16[1,512,4,128]{3,2,1,0:T(4,128)(2,1)S(1)} %constant_dynamic-slice_fusion.5, bf16[1536,128]{1,0:T(8,128)(2,1)} %get-tuple-element.221), kind=kOutput, calls=%fused_computation.58.clone.1 | convolution fusion | flops 824182272 | bytes 8003584 | tf_op jit(solution)/shard_map/while/body/eval_jaxpr/sub | solution.py:67
  96.2 5.0 %fusion.61 = bf16[512,4,128]{0,2,1:T(8,128)(2,1)S(1)} fusion(bf16[4,512,1536]{2,1,0:T(8,128)(2,1)} %get-tuple-element.191, f32[512,4]{0,1:T(4,128)S(1)} %bitcast.148, bf16[1536,128]{0,1:T(8,128)(2,1)} %get-tuple-element.222), kind=kOutput, calls=%fused_computation.18.clone.1 | convolution fusion | flops 805830656 | bytes 7217152 | tf_op jit(solution)/shard_map/while/body/eval_jaxpr/hqk,kd->qhd/dot_general | solution.py:69
  101.2 0.2 copy.82
  101.5 0.7 broadcast_compare_fusion.2
  102.1 0.4 compare_and_fusion.2
  102.5 0.7 iota_compare_fusion.3
  103.2 0.3 pad_add_fusion.2
  103.6 0.2 constant_dynamic-slice_fusion.5
  103.8 9.5 %fusion.60 = (f32[4,512]{1,0:T(4,128)S(1)}, bf16[4,512,1536]{2,1,0:T(8,128)(2,1)}) fusion(pred[512,1536]{1,0:T(8,128)(4,1)S(1)} %pad_add_fusion.2, bf16[1,512,4,128]{3,2,1,0:T(4,128)(2,1)S(1)} %constant_dynamic-slice_fusion.5, bf16[1536,128]{1,0:T(8,128)(2,1)} %get-tuple-element.221), kind=kOutput, calls=%fused_computation.58.clone.1 | convolution fusion | flops 824182272 | bytes 8003584 | tf_op jit(solution)/shard_map/while/body/eval_jaxpr/sub | solution.py:67
  113.2 5.0 %fusion.61 = bf16[512,4,128]{0,2,1:T(8,128)(2,1)S(1)} fusion(bf16[4,512,1536]{2,1,0:T(8,128)(2,1)} %get-tuple-element.191, f32[512,4]{0,1:T(4,128)S(1)} %bitcast.148, bf16[1536,128]{0,1:T(8,128)(2,1)} %get-tuple-element.222), kind=kOutput, calls=%fused_computation.18.clone.1 | convolution fusion | flops 805830656 | bytes 7217152 | tf_op jit(solution)/shard_map/while/body/eval_jaxpr/hqk,kd->qhd/dot_general | solution.py:69
  118.2 0.2 copy.82
  118.5 0.5 broadcast.78
  119.0 1.5 reduce
  120.4 0.8 reshape.95
  121.2 31.5 %all_to_all.102 = bf16[16,2,16384]{2,1,0:T(2,128)(2,1)S(1)} all-to-all(bf16[16,2,16384]{2,1,0:T(2,128)(2,1)S(1)} %reshape.95), channel_id=1, replica_groups=mesh['groups'=2,'ctx'=16] {'ctx'}, dimensions={0} | all-to-all | bytes 2097152 | tf_op jit(solution)/shard_map/all_to_all | solution.py:86
  152.7 1.0 reshape.96
  153.7 0.3 copy.53
  154.0 1.1 copy.59
  (13 shorter events, 0.2 us)
Async XLA Ops:
  0.0 21.1 %copy-start = (bf16[64,1024]{1,0:T(8,128)(2,1)S(1)}, bf16[64,1024]{1,0:T(8,128)(2,1)}, u32[]{:S(2)}) copy-start(bf16[64,1024]{1,0:T(8,128)(2,1)} %param.12) | copy-start | bytes 393220
  0.0 61.3 %copy-start.1 = (s32[32]{0:T(128)S(1)}, s32[32]{0:T(128)}, u32[]{:S(2)}) copy-start(s32[32]{0:T(128)} %param.17) | copy-start | bytes 388
  1.6 15.3 %all-to-all-start.3 = ((bf16[32,16,128]{2,0,1:T(8,128)(2,1)}), bf16[32,16,128]{2,0,1:T(8,128)(2,1)S(1)}, u32[]{:S(2)}, u32[]{:S(2)}) async-start(bf16[32,16,128]{2,0,1:T(8,128)(2,1)} %bitcast.12), calls=%async_computation.3 | async-start | bytes 262144 | tf_op jit(solution)/shard_map/all_to_all | solution.py:40
  17.6 11.4 %all-to-all-start.1 = ((bf16[32,16,128]{2,0,1:T(8,128)(2,1)}), bf16[32,16,128]{2,0,1:T(8,128)(2,1)S(1)}, u32[]{:S(2)}, u32[]{:S(2)}) async-start(bf16[32,16,128]{2,0,1:T(8,128)(2,1)} %bitcast.3), calls=%async_computation.1 | async-start | bytes 262144 | tf_op jit(solution)/shard_map/all_to_all | solution.py:39
  29.7 13.5 %all-to-all-start.4 = ((bf16[64,16,128]{2,0,1:T(8,128)(2,1)}), bf16[64,16,128]{2,0,1:T(8,128)(2,1)S(1)}, u32[]{:S(2)}, u32[]{:S(2)}) async-start(bf16[64,16,128]{2,0,1:T(8,128)(2,1)} %bitcast.16), calls=%async_computation.4 | async-start | bytes 524288 | tf_op jit(solution)/shard_map/all_to_all | solution.py:38
  44.0 13.5 %all-to-all-start.2 = ((bf16[64,16,128]{2,0,1:T(8,128)(2,1)}), bf16[64,16,128]{2,0,1:T(8,128)(2,1)S(1)}, u32[]{:S(2)}, u32[]{:S(2)}) async-start(bf16[64,16,128]{2,0,1:T(8,128)(2,1)} %bitcast.7), calls=%async_computation.2 | async-start | bytes 524288 | tf_op jit(solution)/shard_map/all_to_all | solution.py:37
  57.6 26.6 %all-to-all-start = ((bf16[64,16,512]{2,0,1:T(8,128)(2,1)}), bf16[64,16,512]{2,0,1:T(8,128)(2,1)S(1)}, u32[]{:S(2)}, u32[]{:S(2)}) async-start(bf16[64,16,512]{2,0,1:T(8,128)(2,1)} %bitcast.119), calls=%async_computation | async-start | bytes 2097152 | tf_op jit(solution)/shard_map/all_to_all | solution.py:36
where the time goes:
time: 156 us; the launch traced here: 155 us
  waiting for transfers between devices  52.7 us (34%)
  blocking collectives  31.5 us (20%)
  matrix products  28.8 us (18%)
  starting transfers between devices  21.6 us (14%)
  local copies, waits for them, and re-layouts  13.7 us (9%)
  other arithmetic  6.47 us (4%)
    all_to_all x1, blocking collectives, local(): lax.all_to_all(outputs, 'ctx', split_axis=0, concat_axis=1, tiled=True)  31.5 us
    all_to_all x1, waiting for transfers between devices, local(): lax.all_to_all(q_send, 'ctx', split_axis=1, concat_axis=0, tiled=True)  21 us
    sub x2, matrix products, head_block(): weights = jnp.where(visible[None], jnp.exp(scores - largest), 0.0)  18.9 us
    dot_general x2, matrix products, head_block(): jnp.einsum('hqk,kd->qhd', weights.astype(jnp.bfloat16), value_stack, pref...  9.91 us
    all_to_all x1, waiting for transfers between devices, local(): lax.all_to_all(widen(v_span), 'ctx', split_axis=1, concat_axis=0, tiled=T...  9.07 us
    all_to_all x1, waiting for transfers between devices, local(): lax.all_to_all(widen(k_prefix), 'ctx', split_axis=1, concat_axis=0, tiled...  7.86 us
    all_to_all x1, waiting for transfers between devices, local(): lax.all_to_all(widen(k_span), 'ctx', split_axis=1, concat_axis=0, tiled=T...  7.69 us
    all_to_all x1, starting transfers between devices, local(): lax.all_to_all(widen(v_prefix), 'ctx', split_axis=1, concat_axis=0, tiled...  7.39 us
  transfers between devices with their start and end apart: 5, of which 5 were waited for; matrix products, arithmetic and copies ran while one was open for 4% of the time, Pallas kernels for 0%

commit v1 on v0

v1 whole, which is shorter than its diff:
```python
import functools
import math

import jax
import jax.numpy as jnp
from jax import lax
from jax.experimental import pallas as pl
from jax.experimental.pallas import tpu as pltpu
from jax.sharding import PartitionSpec as P

HD = 128
CORES = 2
NEG_FILL = -1e30
F32 = jnp.float32
BF16 = jnp.bfloat16


def kernel(chips, lanes, q_hbm, k_hbm, v_hbm, kp_hbm, vp_hbm, start_ref, plen_ref, order_ref,
           out_ref, buf, q_in, q_t, acc, top, tot, bias,
           in_sem, ring_send, ring_recv, sib_send, sib_recv):
    rows_span = k_hbm.shape[0]
    rows_pre = kp_hbm.shape[0]
    rows = rows_span + rows_pre
    block_rows = rows_span // 2
    heads_half = buf.shape[-1] // HD
    group = q_hbm.shape[1] // k_hbm.shape[1]
    width = group * rows_span
    rate = math.log2(math.e) / math.sqrt(HD)
    depth = chips // lanes

    me = lax.axis_index("ctx")
    chip, core = lax.div(me, CORES), lax.rem(me, CORES)
    other = 1 - core

    def chip_of(place):
        if lanes == 1:
            return place
        side = lax.div(place, depth)
        along = (1 - side) * place + side * (2 * depth - 1 - place)
        return along * 2 + side

    if lanes == 1:
        place = chip
    else:
        along, side = lax.div(chip, 2), lax.rem(chip, 2)
        place = (1 - side) * along + side * (2 * depth - 1 - along)
    after = chip_of(lax.rem(place + 1, chips)) * CORES + core
    before = chip_of(lax.rem(place + chips - 1, chips)) * CORES + core
    sibling = chip * CORES + other
    onward = (after, before)

    def origin(half, step):
        return lax.rem(place + (chips - step if half == 0 else step), chips)

    half_cols = buf.shape[-1]
    loads = []
    for kv, (span, pre) in enumerate(((k_hbm, kp_hbm), (v_hbm, vp_hbm))):
        for half in range(2):
            cols = pl.ds(half * half_cols, half_cols)
            for part, (src, at, size) in enumerate(((span, 0, rows_span), (pre, rows_span, rows_pre))):
                copy = pltpu.make_async_copy(
                    src.at[:, cols],
                    buf.at[half, place, kv, core, pl.ds(at, size)],
                    in_sem.at[kv * 4 + half * 2 + part],
                )
                copy.start()
                loads.append(copy)
    q_load = pltpu.make_async_copy(q_hbm, q_in, in_sem.at[8])
    q_load.start()

    barrier = pltpu.get_barrier_semaphore()
    for peer in (after, before, sibling):
        pl.semaphore_signal(barrier, inc=1, device_id={"ctx": peer}, device_id_type=pl.DeviceIdType.MESH)
    pl.semaphore_wait(barrier, 3)

    def ring(half, step, kv):
        piece = buf.at[half, origin(half, step), kv, core]
        return pltpu.make_async_remote_copy(
            src_ref=piece, dst_ref=piece,
            send_sem=ring_send.at[half, step, kv], recv_sem=ring_recv.at[half, step, kv],
            device_id={"ctx": onward[half]}, device_id_type=pl.DeviceIdType.MESH)

    def across(half, step, kv):
        piece = buf.at[half, origin(half, step), kv, core]
        return pltpu.make_async_remote_copy(
            src_ref=piece, dst_ref=piece,
            send_sem=sib_send.at[half, step, kv], recv_sem=sib_recv.at[half, step, kv],
            device_id={"ctx": sibling}, device_id_type=pl.DeviceIdType.MESH)

    def ring_arrival(half, step, kv):
        piece = buf.at[half, origin(half, step), kv, core]
        return pltpu.make_async_remote_copy(
            src_ref=piece, dst_ref=piece,
            send_sem=ring_send.at[half, step - 1, kv], recv_sem=ring_recv.at[half, step - 1, kv],
            device_id={"ctx": onward[half]}, device_id_type=pl.DeviceIdType.MESH)

    def across_arrival(half, step, kv):
        piece = buf.at[half, origin(half, step), kv, other]
        return pltpu.make_async_remote_copy(
            src_ref=piece, dst_ref=piece,
            send_sem=sib_send.at[half, step, kv], recv_sem=sib_recv.at[half, step, kv],
            device_id={"ctx": sibling}, device_id_type=pl.DeviceIdType.MESH)

    for kv in range(2):
        for half in range(2):
            for part in range(2):
                loads[kv * 4 + half * 2 + part].wait()
            ring(half, 0, kv).start()
    for kv in range(2):
        for half in range(2):
            across(half, 0, kv).start()

    q_load.wait()
    for head in range(2 * heads_half):
        stacked = jnp.concatenate(
            [q_in[:, (head * group + g) * HD:(head * group + g + 1) * HD] for g in range(group)], 0)
        q_t[head] = stacked.T
    acc[...] = jnp.zeros_like(acc)
    tot[...] = jnp.zeros_like(tot)
    top[...] = jnp.full_like(top, NEG_FILL)

    start = start_ref[0]
    plen = plen_ref[0]

    def positions(shape, device, axis):
        index = lax.broadcasted_iota(jnp.int32, shape, axis)
        if axis == 1:
            index = lax.rem(index, rows_span)
        first = order_ref[device * 2] * block_rows
        second = order_ref[device * 2 + 1] * block_rows
        return jnp.where(index < block_rows, first + index, second + index - block_rows)

    rep = 2 * rows_span
    q_pos = positions((1, rep), me, 1)

    def attend(half, step):
        for kv in range(2):
            across_arrival(half, step, kv).wait_recv()
        at = origin(half, step)
        source = chip_of(at)
        for c in range(CORES):
            device = source * CORES + c
            k_pos = positions((rows_span, rep), device, 0)
            seen = (k_pos <= q_pos) & (k_pos >= start)
            bias[c * rows:c * rows + rows_span] = jnp.where(seen, 0.0, NEG_FILL).astype(F32)
            slot = device * rows_pre + lax.broadcasted_iota(jnp.int32, (rows_pre, rep), 0)
            bias[c * rows + rows_span:(c + 1) * rows] = jnp.where(slot < plen, 0.0, NEG_FILL).astype(F32)
        shade = jnp.concatenate([bias[...]] * (width // rep), 1)
        for j in range(heads_half):
            head = half * heads_half + j
            cols = slice(j * HD, (j + 1) * HD)
            keys = buf[half, at, 0, :, :, cols].reshape(CORES * rows, HD)
            values = buf[half, at, 1, :, :, cols].reshape(CORES * rows, HD)
            score = jnp.dot(keys, q_t[head], preferred_element_type=F32) + shade
            old = top[head]
            new = jnp.maximum(old, jnp.max(score, axis=0, keepdims=True))
            shrink = jnp.exp2((old - new) * rate)
            weight = jnp.exp2((score - new) * rate)
            tot[head] = tot[head] * shrink + jnp.sum(weight, axis=0, keepdims=True)
            top[head] = new
            acc[head] = acc[head] * shrink + lax.dot_general(
                values, weight.astype(BF16), (((0,), (0,)), ((), ())), preferred_element_type=F32)

    def body(step, carry):
        for kv in range(2):
            for half in range(2):
                ring_arrival(half, step, kv).wait_recv()

                @pl.when(step < chips - 1)
                def _():
                    ring(half, step, kv).start()

                across(half, step, kv).start()
            attend(kv, step - 1)
        return carry

    lax.fori_loop(1, chips, body, 0)
    for half in range(2):
        attend(half, jnp.int32(chips - 1))

    for head in range(2 * heads_half):
        done = (acc[head] / tot[head]).T.astype(BF16)
        for g in range(group):
            out_ref[:, (head * group + g) * HD:(head * group + g + 1) * HD] = done[g * rows_span:(g + 1) * rows_span]

    def drain(step, carry):
        for kv in range(2):
            for half in range(2):
                across(half, step, kv).wait_send()

                @pl.when(step < chips - 1)
                def _():
                    ring(half, step, kv).wait_send()
        return carry

    lax.fori_loop(0, chips, drain, 0)


def local(chips, lanes, q_span, k_span, v_span, k_prefix, v_prefix, start_offset, prefix_len, block_order):
    rows_span, cols = k_span.shape
    rows = rows_span + k_prefix.shape[0]
    heads = cols // HD
    width = q_span.shape[1] // cols * rows_span
    steps = chips
    hbm = pl.BlockSpec(memory_space=pltpu.HBM)
    smem = pl.BlockSpec(memory_space=pltpu.SMEM)
    sems = pltpu.SemaphoreType.DMA((2, steps, 2))
    ops = heads * width * rows * CORES * chips
    return pl.pallas_call(
        functools.partial(kernel, chips, lanes),
        out_shape=jax.ShapeDtypeStruct(q_span.shape, BF16),
        in_specs=[hbm] * 5 + [smem] * 3,
        out_specs=pl.BlockSpec(memory_space=pltpu.VMEM),
        scratch_shapes=[
            pltpu.VMEM((2, chips, 2, CORES, rows, cols // 2), BF16),
            pltpu.VMEM(q_span.shape, BF16),
            pltpu.VMEM((heads, HD, width), BF16),
            pltpu.VMEM((heads, HD, width), F32),
            pltpu.VMEM((heads, 1, width), F32),
            pltpu.VMEM((heads, 1, width), F32),
            pltpu.VMEM((CORES * rows, 2 * rows_span), F32),
            pltpu.SemaphoreType.DMA((9,)),
            sems, sems, sems, sems,
        ],
        compiler_params=pltpu.CompilerParams(
            collective_id=0, has_side_effects=True, vmem_limit_bytes=48 * 1024 * 1024),
        cost_estimate=pl.CostEstimate(flops=4 * HD * ops, bytes_accessed=4 * q_span.size, transcendentals=ops),
    )(q_span, k_span, v_span, k_prefix, v_prefix, start_offset, prefix_len, block_order)


def solution(mesh):
    chips = mesh.shape["ctx"] // CORES
    lanes = 2 if mesh.shape["groups"] == 2 and chips % 2 == 0 else 1
    rows = P(("groups", "ctx"), None)
    one = P("groups")
    return jax.shard_map(
        functools.partial(local, chips, lanes), mesh=mesh,
        in_specs=(rows,) * 5 + (one,) * 3, out_specs=rows, check_vma=False
    )
```

time: 156 us -> 50.4 us (0.32)
  waiting for transfers between devices: 52.7 us -> 0 us
  Pallas kernels: 0 us -> 43.1 us
  blocking collectives: 31.5 us -> 0 us
  matrix products: 28.8 us -> 0 us
  starting transfers between devices: 21.6 us -> 0 us
  local copies, waits for them, and re-layouts: 13.7 us -> 5.68 us
  other arithmetic: 6.47 us -> 0 us
    all_to_all x5 -> x0, waiting for transfers between devices: 52.7 us -> none  [the longest x1 21 us: local(): lax.all_to_all(q_send, 'ctx', split_axis=1, concat_axis=0, tiled=True)]
    pallas_call x0 -> x1, Pallas kernels: none -> 43.1 us  [local(): pl.pallas_call(functools.partial(kernel, chips, lanes), out_shape=jax.Sha...]
    all_to_all x1 -> x0, blocking collectives: 31.5 us -> none  [local(): lax.all_to_all(outputs, 'ctx', split_axis=0, concat_axis=1, tiled=True)]
    all_to_all x5 -> x0, starting transfers between devices: 21.6 us -> none  [the longest x1 7.39 us: local(): lax.all_to_all(widen(v_prefix), 'ctx', split_axis=1, concat_axis=0, tiled...]
    sub x2 -> x0, matrix products: 18.9 us -> none  [head_block(): weights = jnp.where(visible[None], jnp.exp(scores - largest), 0.0)]
    dot_general x2 -> x0, matrix products: 9.91 us -> none  [head_block(): jnp.einsum('hqk,kd->qhd', weights.astype(jnp.bfloat16), value_stack, pref...]
    broadcast_in_dim x8 -> x0, local copies, waits for them, and re-layouts: 5.54 us -> none  [widen(): jnp.broadcast_to(source.reshape(length, kv_heads, 1, HD), (length, kv_hea...]
    reshape x3 -> x0, local copies, waits for them, and re-layouts: 3.09 us -> none  [the longest x1 2.31 us: local(): q_send = q_span.reshape(local_rows, members, heads_here * HD)]
  transfers between devices with their start and end apart: 5 -> 0, of which waited for: 5 -> 0; matrix products, arithmetic and copies ran while one was open for 4% -> 0% of each run, Pallas kernels for 0% -> 0%
where the time goes in v1:
time: 50.4 us; the launch traced here: 50.1 us
  Pallas kernels  43.1 us (86%)
  local copies, waits for them, and re-layouts  5.68 us (11%)
  between operations  1.35 us (3%)
    pallas_call x1, Pallas kernels, local(): pl.pallas_call(functools.partial(kernel, chips, lanes), out_shape=jax.Sha...  43.1 us
    unnamed x13, local copies, waits for them, and re-layouts  5.68 us

profile of v1, /device:TPU:0, one launch (start us, length us, event | category | flops | bytes accessed | tf_op | source)
XLA Modules:
  0.0 50.1 jit_solution(11681432887248312899)
XLA Ops:
  0.7 0.0 copy-start.5
  1.3 0.0 copy-done.5
  1.3 0.0 copy-start
  1.3 1.2 %copy-done = bf16[64,8192]{1,0:T(8,128)(2,1)S(1)} copy-done((bf16[64,8192]{1,0:T(8,128)(2,1)S(1)}, bf16[64,8192]{1,0:T(8,128)(2,1)}, u32[]{:S(2)}) %copy-start) | copy-done | bytes 1048600
  2.6 0.0 copy-start.1
  2.6 0.9 %copy-done.1 = bf16[64,1024]{1,0:T(8,128)(2,1)S(1)} copy-done((bf16[64,1024]{1,0:T(8,128)(2,1)S(1)}, bf16[64,1024]{1,0:T(8,128)(2,1)}, u32[]{:S(2)}) %copy-start.1) | copy-done | bytes 131096
  3.5 0.0 copy-start.2
  3.5 0.9 %copy-done.2 = bf16[64,1024]{1,0:T(8,128)(2,1)S(1)} copy-done((bf16[64,1024]{1,0:T(8,128)(2,1)S(1)}, bf16[64,1024]{1,0:T(8,128)(2,1)}, u32[]{:S(2)}) %copy-start.2) | copy-done | bytes 131096
  4.4 0.0 copy-start.3
  4.4 0.8 %copy-done.3 = bf16[32,1024]{1,0:T(8,128)(2,1)S(1)} copy-done((bf16[32,1024]{1,0:T(8,128)(2,1)S(1)}, bf16[32,1024]{1,0:T(8,128)(2,1)}, u32[]{:S(2)}) %copy-start.3) | copy-done | bytes 65560
  5.2 0.0 copy-start.4
  5.2 0.8 %copy-done.4 = bf16[32,1024]{1,0:T(8,128)(2,1)S(1)} copy-done((bf16[32,1024]{1,0:T(8,128)(2,1)S(1)}, bf16[32,1024]{1,0:T(8,128)(2,1)}, u32[]{:S(2)}) %copy-start.4) | copy-done | bytes 65560
  6.0 43.1 %shard_map.82 = bf16[64,8192]{1,0:T(8,128)(2,1)S(1)} custom-call(bf16[64,8192]{1,0:T(8,128)(2,1)S(1)} %copy-done, bf16[64,1024]{1,0:T(8,128)(2,1)S(1)} %copy-done.1, bf16[64,1024]{1,0:T(8,128)(2,1)S(1)} %copy-done.2, bf16[32,1024]{1,0:T(8,128)(2,1)S(1)} %copy-done.3, bf16[32,1024]{1,0:T(8,128)(2,1)S(1)} %copy-done.4, s32[1]{0:T(128)S(6)} %copy.10.start_ref, ...), custom_call_target="tpu_custom_call" | custom-call | flops 3221225472 | bytes 2097152 | tf_op jit(solution)/shard_map/pallas_call | solution.py:209
  49.2 1.0 %copy.12 = bf16[64,8192]{1,0:T(8,128)(2,1)} copy(bf16[64,8192]{1,0:T(8,128)(2,1)S(1)} %shard_map.82) | data formatting | bytes 2097152
Async XLA Ops:
  0.7 0.7 %copy-start.5 = (s32[32]{0:T(128)S(1)}, s32[32]{0:T(128)}, u32[]{:S(2)}) copy-start(s32[32]{0:T(128)} %order_ref.1) | copy-start | bytes 388
  1.3 1.2 %copy-start = (bf16[64,8192]{1,0:T(8,128)(2,1)S(1)}, bf16[64,8192]{1,0:T(8,128)(2,1)}, u32[]{:S(2)}) copy-start(bf16[64,8192]{1,0:T(8,128)(2,1)} %q_hbm.1) | copy-start | bytes 3145732
  2.6 0.9 %copy-start.1 = (bf16[64,1024]{1,0:T(8,128)(2,1)S(1)}, bf16[64,1024]{1,0:T(8,128)(2,1)}, u32[]{:S(2)}) copy-start(bf16[64,1024]{1,0:T(8,128)(2,1)} %k_hbm.1) | copy-start | bytes 393220
  3.5 0.9 %copy-start.2 = (bf16[64,1024]{1,0:T(8,128)(2,1)S(1)}, bf16[64,1024]{1,0:T(8,128)(2,1)}, u32[]{:S(2)}) copy-start(bf16[64,1024]{1,0:T(8,128)(2,1)} %v_hbm.1) | copy-start | bytes 393220
  4.4 0.8 %copy-start.3 = (bf16[32,1024]{1,0:T(8,128)(2,1)S(1)}, bf16[32,1024]{1,0:T(8,128)(2,1)}, u32[]{:S(2)}) copy-start(bf16[32,1024]{1,0:T(8,128)(2,1)} %kp_hbm.1) | copy-start | bytes 196612
  5.2 0.8 %copy-start.4 = (bf16[32,1024]{1,0:T(8,128)(2,1)S(1)}, bf16[32,1024]{1,0:T(8,128)(2,1)}, u32[]{:S(2)}) copy-start(bf16[32,1024]{1,0:T(8,128)(2,1)} %vp_hbm.1) | copy-start | bytes 196612

commit v2 on v1

--- a/solution.py
+++ b/solution.py
@@ -223,7 +223,7 @@
             sems, sems, sems, sems,
         ],
         compiler_params=pltpu.CompilerParams(
-            collective_id=0, has_side_effects=True, vmem_limit_bytes=48 * 1024 * 1024),
+            collective_id=0, has_side_effects=True, vmem_limit_bytes=63 * 1024 * 1024),
         cost_estimate=pl.CostEstimate(flops=4 * HD * ops, bytes_accessed=4 * q_span.size, transcendentals=ops),
     )(q_span, k_span, v_span, k_prefix, v_prefix, start_offset, prefix_len, block_order)
 

time: 50.4 us -> 47.9 us (0.950)
  local copies, waits for them, and re-layouts: 5.68 us -> 2.26 us
  Pallas kernels: 43.1 us -> 44.1 us
    unnamed x13 -> x1, local copies, waits for them, and re-layouts: 5.68 us -> 2.26 us
    pallas_call x1, Pallas kernels: 43.1 us -> 44.1 us  [local(): pl.pallas_call(functools.partial(kernel, chips, lanes), out_shape=jax.Sha...]
where the time goes in v2:
time: 47.9 us; the launch traced here: 47.7 us
  Pallas kernels  44.1 us (92%)
  local copies, waits for them, and re-layouts  2.26 us (5%)
  between operations  1.3 us (3%)
    pallas_call x1, Pallas kernels, local(): pl.pallas_call(functools.partial(kernel, chips, lanes), out_shape=jax.Sha...  44.1 us
    unnamed x1, local copies, waits for them, and re-layouts  2.26 us

profile of v2, /device:TPU:0, one launch (start us, length us, event | category | flops | bytes accessed | tf_op | source)
XLA Modules:
  0.0 47.7 jit_solution(15895024078753602567)
XLA Ops:
  1.3 44.1 %shard_map.82 = bf16[64,8192]{1,0:T(8,128)(2,1)} custom-call(bf16[64,8192]{1,0:T(8,128)(2,1)} %q_hbm.1, bf16[64,1024]{1,0:T(8,128)(2,1)} %k_hbm.1, bf16[64,1024]{1,0:T(8,128)(2,1)} %v_hbm.1, bf16[32,1024]{1,0:T(8,128)(2,1)} %kp_hbm.1, bf16[32,1024]{1,0:T(8,128)(2,1)} %vp_hbm.1, s32[1]{0:T(128)S(6)} %copy.10.start_ref, s32[1]{0:T(128)S(6)} %copy.11.plen_ref, ...), custom_call_target="tpu_custom_call" | custom-call | flops 3221225472 | bytes 2097152 | tf_op jit(solution)/shard_map/pallas_call | solution.py:209
  45.4 2.3 %copy.12 = bf16[64,8192]{1,0:T(8,128)(2,1)} copy(bf16[64,8192]{1,0:T(8,128)(2,1)} %shard_map.82) | data formatting | bytes 2097152

commit v3 on v2

--- a/solution.py
+++ b/solution.py
@@ -49,8 +49,12 @@
     sibling = chip * CORES + other
     onward = (after, before)
 
-    def origin(half, step):
-        return lax.rem(place + (chips - step if half == 0 else step), chips)
+    def origin(way, step):
+        return lax.rem(place + (chips - step if way == 0 else step), chips)
+
+    def piece(way, step, turn, holder):
+        half = way if turn < 2 else 1 - way
+        return buf.at[half, origin(way, step), turn % 2, holder]
 
     half_cols = buf.shape[-1]
     loads = []
@@ -73,42 +77,34 @@
         pl.semaphore_signal(barrier, inc=1, device_id={"ctx": peer}, device_id_type=pl.DeviceIdType.MESH)
     pl.semaphore_wait(barrier, 3)
 
-    def ring(half, step, kv):
-        piece = buf.at[half, origin(half, step), kv, core]
+    def move(ref, step, way, turn, sends, recvs, peer):
         return pltpu.make_async_remote_copy(
-            src_ref=piece, dst_ref=piece,
-            send_sem=ring_send.at[half, step, kv], recv_sem=ring_recv.at[half, step, kv],
-            device_id={"ctx": onward[half]}, device_id_type=pl.DeviceIdType.MESH)
-
-    def across(half, step, kv):
-        piece = buf.at[half, origin(half, step), kv, core]
-        return pltpu.make_async_remote_copy(
-            src_ref=piece, dst_ref=piece,
-            send_sem=sib_send.at[half, step, kv], recv_sem=sib_recv.at[half, step, kv],
-            device_id={"ctx": sibling}, device_id_type=pl.DeviceIdType.MESH)
-
-    def ring_arrival(half, step, kv):
-        piece = buf.at[half, origin(half, step), kv, core]
-        return pltpu.make_async_remote_copy(
-            src_ref=piece, dst_ref=piece,
-            send_sem=ring_send.at[half, step - 1, kv], recv_sem=ring_recv.at[half, step - 1, kv],
-            device_id={"ctx": onward[half]}, device_id_type=pl.DeviceIdType.MESH)
-
-    def across_arrival(half, step, kv):
-        piece = buf.at[half, origin(half, step), kv, other]
-        return pltpu.make_async_remote_copy(
-            src_ref=piece, dst_ref=piece,
-            send_sem=sib_send.at[half, step, kv], recv_sem=sib_recv.at[half, step, kv],
-            device_id={"ctx": sibling}, device_id_type=pl.DeviceIdType.MESH)
-
-    for kv in range(2):
-        for half in range(2):
-            for part in range(2):
-                loads[kv * 4 + half * 2 + part].wait()
-            ring(half, 0, kv).start()
-    for kv in range(2):
-        for half in range(2):
-            across(half, 0, kv).start()
+            src_ref=ref, dst_ref=ref,
+            send_sem=sends.at[way, step, turn], recv_sem=recvs.at[way, step, turn],
+            device_id={"ctx": peer}, device_id_type=pl.DeviceIdType.MESH)
+
+    def ring(way, step, turn):
+        return move(piece(way, step, turn, core), step, way, turn, ring_send, ring_recv, onward[way])
+
+    def ring_arrival(way, step, turn):
+        return move(piece(way, step, turn, core), step - 1, way, turn, ring_send, ring_recv, onward[way])
+
+    def across(way, step, turn):
+        return move(piece(way, step, turn, core), step, way, turn, sib_send, sib_recv, sibling)
+
+    def across_arrival(way, step, turn):
+        return move(piece(way, step, turn, other), step, way, turn, sib_send, sib_recv, sibling)
+
+    for turn in range(4):
+        for way in range(2):
+            half = way if turn < 2 else 1 - way
+            if turn < 2:
+                for part in range(2):
+                    loads[turn * 4 + half * 2 + part].wait()
+            ring(way, 0, turn).start()
+    for turn in (2, 3):
+        for way in range(2):
+            across(way, 0, turn).start()
 
     q_load.wait()
     for head in range(2 * heads_half):
@@ -133,10 +129,11 @@
     rep = 2 * rows_span
     q_pos = positions((1, rep), me, 1)
 
-    def attend(half, step):
+    def attend(way, step, late, last=False):
+        half = 1 - way if late else way
         for kv in range(2):
-            across_arrival(half, step, kv).wait_recv()
-        at = origin(half, step)
+            across_arrival(way, step, 2 * late + kv).wait_recv()
+        at = origin(way, step)
         source = chip_of(at)
         for c in range(CORES):
             device = source * CORES + c
@@ -156,44 +153,70 @@
             new = jnp.maximum(old, jnp.max(score, axis=0, keepdims=True))
             shrink = jnp.exp2((old - new) * rate)
             weight = jnp.exp2((score - new) * rate)
-            tot[head] = tot[head] * shrink + jnp.sum(weight, axis=0, keepdims=True)
-            top[head] = new
-            acc[head] = acc[head] * shrink + lax.dot_general(
+            total = tot[head] * shrink + jnp.sum(weight, axis=0, keepdims=True)
+            summed = acc[head] * shrink + lax.dot_general(
                 values, weight.astype(BF16), (((0,), (0,)), ((), ())), preferred_element_type=F32)
+            if last:
+                done = (summed * (1.0 / total)).T.astype(BF16)
+                for g in range(group):
+                    out_ref[:, (head * group + g) * HD:(head * group + g + 1) * HD] = (
+                        done[g * rows_span:(g + 1) * rows_span])
+            else:
+                tot[head] = total
+                top[head] = new
+                acc[head] = summed
+
+    hops = chips // 2
 
     def body(step, carry):
-        for kv in range(2):
-            for half in range(2):
-                ring_arrival(half, step, kv).wait_recv()
-
-                @pl.when(step < chips - 1)
-                def _():
-                    ring(half, step, kv).start()
-
-                across(half, step, kv).start()
-            attend(kv, step - 1)
+        for turn in range(4):
+            for way in range(2):
+                ring_arrival(way, step, turn).wait_recv()
+                if turn < 2:
+                    ring(way, step, turn).start()
+                else:
+                    @pl.when(step < hops - 1)
+                    def _():
+                        ring(way, step, turn).start()
+
+                across(way, step, turn).start()
+            if turn < 2:
+                attend(turn, step - 1, 1)
+            else:
+                attend(turn - 2, step, 0)
         return carry
 
-    lax.fori_loop(1, chips, body, 0)
-    for half in range(2):
-        attend(half, jnp.int32(chips - 1))
-
-    for head in range(2 * heads_half):
-        done = (acc[head] / tot[head]).T.astype(BF16)
-        for g in range(group):
-            out_ref[:, (head * group + g) * HD:(head * group + g + 1) * HD] = done[g * rows_span:(g + 1) * rows_span]
+    lax.fori_loop(1, hops, body, 0)
+    end = jnp.int32(hops)
+    for turn in range(2):
+        for way in range(2):
+            ring_arrival(way, end, turn).wait_recv()
+            across(way, end, turn).start()
+        attend(turn, end - 1, 1)
+    for way in range(2):
+        attend(way, end, 0, True)
 
     def drain(step, carry):
-        for kv in range(2):
-            for half in range(2):
-                across(half, step, kv).wait_send()
-
-                @pl.when(step < chips - 1)
-                def _():
-                    ring(half, step, kv).wait_send()
+        for turn in range(4):
+            for way in range(2):
+                if turn < 2:
+                    ring(way, step, turn).wait_send()
+
+                    @pl.when(step > 0)
+                    def _():
+                        across(way, step, turn).wait_send()
+                else:
+                    across(way, step, turn).wait_send()
+
+                    @pl.when(step < hops - 1)
+                    def _():
+                        ring(way, step, turn).wait_send()
         return carry
 
-    lax.fori_loop(0, chips, drain, 0)
+    lax.fori_loop(0, hops, drain, 0)
+    for turn in range(2):
+        for way in range(2):
+            across(way, end, turn).wait_send()
 
 
 def local(chips, lanes, q_span, k_span, v_span, k_prefix, v_prefix, start_offset, prefix_len, block_order):
@@ -201,10 +224,10 @@
     rows = rows_span + k_prefix.shape[0]
     heads = cols // HD
     width = q_span.shape[1] // cols * rows_span
-    steps = chips
+    steps = chips // 2 + 1
     hbm = pl.BlockSpec(memory_space=pltpu.HBM)
     smem = pl.BlockSpec(memory_space=pltpu.SMEM)
-    sems = pltpu.SemaphoreType.DMA((2, steps, 2))
+    sems = pltpu.SemaphoreType.DMA((2, steps, 4))
     ops = heads * width * rows * CORES * chips
     return pl.pallas_call(
         functools.partial(kernel, chips, lanes),

time: 47.9 us -> 46 us (0.960)
  Pallas kernels: 44.1 us -> 42.2 us
    pallas_call x1, Pallas kernels: 44.1 us -> 42.2 us  [local(): pl.pallas_call(functools.partial(kernel, chips, lanes), out_shape=jax.Sha...]
where the time goes in v3:
time: 46 us; the launch traced here: 45.8 us
  Pallas kernels  42.2 us (92%)
  local copies, waits for them, and re-layouts  2.26 us (5%)
  between operations  1.3 us (3%)
    pallas_call x1, Pallas kernels, local(): pl.pallas_call(functools.partial(kernel, chips, lanes), out_shape=jax.Sha...  42.2 us
    unnamed x1, local copies, waits for them, and re-layouts  2.26 us

profile of v3, /device:TPU:0, one launch (start us, length us, event | category | flops | bytes accessed | tf_op | source)
XLA Modules:
  0.0 45.8 jit_solution(14564728186022905354)
XLA Ops:
  1.3 42.2 %shard_map.82 = bf16[64,8192]{1,0:T(8,128)(2,1)} custom-call(bf16[64,8192]{1,0:T(8,128)(2,1)} %q_hbm.1, bf16[64,1024]{1,0:T(8,128)(2,1)} %k_hbm.1, bf16[64,1024]{1,0:T(8,128)(2,1)} %v_hbm.1, bf16[32,1024]{1,0:T(8,128)(2,1)} %kp_hbm.1, bf16[32,1024]{1,0:T(8,128)(2,1)} %vp_hbm.1, s32[1]{0:T(128)S(6)} %copy.10.start_ref, s32[1]{0:T(128)S(6)} %copy.11.plen_ref, ...), custom_call_target="tpu_custom_call" | custom-call | flops 3221225472 | bytes 2097152 | tf_op jit(solution)/shard_map/pallas_call | solution.py:232
  43.5 2.3 %copy.12 = bf16[64,8192]{1,0:T(8,128)(2,1)} copy(bf16[64,8192]{1,0:T(8,128)(2,1)} %shard_map.82) | data formatting | bytes 2097152

commit v4 on v3

--- a/solution.py
+++ b/solution.py
@@ -15,9 +15,9 @@
 BF16 = jnp.bfloat16
 
 
-def kernel(chips, lanes, q_hbm, k_hbm, v_hbm, kp_hbm, vp_hbm, start_ref, plen_ref, order_ref,
-           out_ref, buf, q_in, q_t, acc, top, tot, bias,
-           in_sem, ring_send, ring_recv, sib_send, sib_recv):
+def kernel(chips, lanes, q_hbm, k_hbm, v_hbm, kp_hbm, vp_hbm, start_hbm, plen_hbm, order_hbm,
+           out_hbm, start_ref, plen_ref, order_ref, out_ref, buf, q_in, q_t, acc, top, tot, bias,
+           in_sem, num_sem, out_sem, ring_send, ring_recv, sib_send, sib_recv):
     rows_span = k_hbm.shape[0]
     rows_pre = kp_hbm.shape[0]
     rows = rows_span + rows_pre
@@ -55,6 +55,10 @@
     def piece(way, step, turn, holder):
         half = way if turn < 2 else 1 - way
         return buf.at[half, origin(way, step), turn % 2, holder]
+
+    barrier = pltpu.get_barrier_semaphore()
+    for peer in (after, before, sibling):
+        pl.semaphore_signal(barrier, inc=1, device_id={"ctx": peer}, device_id_type=pl.DeviceIdType.MESH)
 
     half_cols = buf.shape[-1]
     loads = []
@@ -72,9 +76,12 @@
     q_load = pltpu.make_async_copy(q_hbm, q_in, in_sem.at[8])
     q_load.start()
 
-    barrier = pltpu.get_barrier_semaphore()
-    for peer in (after, before, sibling):
-        pl.semaphore_signal(barrier, inc=1, device_id={"ctx": peer}, device_id_type=pl.DeviceIdType.MESH)
+    numbers = [
+        pltpu.make_async_copy(src, dst, num_sem.at[i])
+        for i, (src, dst) in enumerate(((start_hbm, start_ref), (plen_hbm, plen_ref), (order_hbm, order_ref)))
+    ]
+    for copy in numbers:
+        copy.start()
     pl.semaphore_wait(barrier, 3)
 
     def move(ref, step, way, turn, sends, recvs, peer):
@@ -115,6 +122,8 @@
     tot[...] = jnp.zeros_like(tot)
     top[...] = jnp.full_like(top, NEG_FILL)
 
+    for copy in numbers:
+        copy.wait()
     start = start_ref[0]
     plen = plen_ref[0]
 
@@ -128,6 +137,10 @@
 
     rep = 2 * rows_span
     q_pos = positions((1, rep), me, 1)
+
+    def store(head):
+        cols = pl.ds(head * group * HD, group * HD)
+        return pltpu.make_async_copy(out_ref.at[:, cols], out_hbm.at[:, cols], out_sem.at[head])
 
     def attend(way, step, late, last=False):
         half = 1 - way if late else way
@@ -161,6 +174,7 @@
                 for g in range(group):
                     out_ref[:, (head * group + g) * HD:(head * group + g + 1) * HD] = (
                         done[g * rows_span:(g + 1) * rows_span])
+                store(head).start()
             else:
                 tot[head] = total
                 top[head] = new
@@ -217,6 +231,8 @@
     for turn in range(2):
         for way in range(2):
             across(way, end, turn).wait_send()
+    for head in range(2 * heads_half):
+        store(head).wait()
 
 
 def local(chips, lanes, q_span, k_span, v_span, k_prefix, v_prefix, start_offset, prefix_len, block_order):
@@ -226,15 +242,18 @@
     width = q_span.shape[1] // cols * rows_span
     steps = chips // 2 + 1
     hbm = pl.BlockSpec(memory_space=pltpu.HBM)
-    smem = pl.BlockSpec(memory_space=pltpu.SMEM)
     sems = pltpu.SemaphoreType.DMA((2, steps, 4))
     ops = heads * width * rows * CORES * chips
     return pl.pallas_call(
         functools.partial(kernel, chips, lanes),
         out_shape=jax.ShapeDtypeStruct(q_span.shape, BF16),
-        in_specs=[hbm] * 5 + [smem] * 3,
-        out_specs=pl.BlockSpec(memory_space=pltpu.VMEM),
+        in_specs=[hbm] * 8,
+        out_specs=hbm,
         scratch_shapes=[
+            pltpu.SMEM(start_offset.shape, jnp.int32),
+            pltpu.SMEM(prefix_len.shape, jnp.int32),
+            pltpu.SMEM(block_order.shape, jnp.int32),
+            pltpu.VMEM(q_span.shape, BF16),
             pltpu.VMEM((2, chips, 2, CORES, rows, cols // 2), BF16),
             pltpu.VMEM(q_span.shape, BF16),
             pltpu.VMEM((heads, HD, width), BF16),
@@ -243,6 +262,8 @@
             pltpu.VMEM((heads, 1, width), F32),
             pltpu.VMEM((CORES * rows, 2 * rows_span), F32),
             pltpu.SemaphoreType.DMA((9,)),
+            pltpu.SemaphoreType.DMA((3,)),
+            pltpu.SemaphoreType.DMA((heads,)),
             sems, sems, sems, sems,
         ],
         compiler_params=pltpu.CompilerParams(

time: 46 us -> 44.9 us (0.976)
  Pallas kernels: 42.2 us -> 41.2 us
    pallas_call x1, Pallas kernels: 42.2 us -> 41.2 us  [local(): pl.pallas_call(functools.partial(kernel, chips, lanes), out_shape=jax.Sha...]
where the time goes in v4:
time: 44.9 us; the launch traced here: 44.8 us
  Pallas kernels  41.2 us (92%)
  local copies, waits for them, and re-layouts  2.26 us (5%)
  between operations  1.3 us (3%)
    pallas_call x1, Pallas kernels, local(): pl.pallas_call(functools.partial(kernel, chips, lanes), out_shape=jax.Sha...  41.2 us
    unnamed x1, local copies, waits for them, and re-layouts  2.26 us

profile of v4, /device:TPU:0, one launch (start us, length us, event | category | flops | bytes accessed | tf_op | source)
XLA Modules:
  0.0 44.8 jit_solution(8962420651047353105)
XLA Ops:
  1.3 41.2 %shard_map.82 = bf16[64,8192]{1,0:T(8,128)(2,1)} custom-call(bf16[64,8192]{1,0:T(8,128)(2,1)} %q_hbm.1, bf16[64,1024]{1,0:T(8,128)(2,1)} %k_hbm.1, bf16[64,1024]{1,0:T(8,128)(2,1)} %v_hbm.1, bf16[32,1024]{1,0:T(8,128)(2,1)} %kp_hbm.1, bf16[32,1024]{1,0:T(8,128)(2,1)} %vp_hbm.1, s32[1]{0:T(128)S(6)} %copy.10.start_hbm, s32[1]{0:T(128)S(6)} %copy.11.plen_hbm, ...), custom_call_target="tpu_custom_call" | custom-call | flops 3221225472 | bytes 2097152 | tf_op jit(solution)/shard_map/pallas_call | solution.py:247
  42.5 2.3 %copy.12 = bf16[64,8192]{1,0:T(8,128)(2,1)} copy(bf16[64,8192]{1,0:T(8,128)(2,1)} %shard_map.82) | data formatting | bytes 2097152
